TPU v7x, 128 devices: a whole 4x4x4 slice. The times are simulated.
128 devices in a mesh: dp: 4 (over x), fsdp: 4 (over z_hi, core), seq: 8 (over z_lo, y).
Axes of the slice: x: 4, y: 4, z: 4 (z_hi: 2, z_lo: 2; z = z_hi * 2 + z_lo), core: 2. Of those that a mesh axis runs over, the one named last changes fastest.
Arguments:
- frames: bfloat16 [16, 2048, 1536], P(('dp', 'fsdp'), 'seq'), may hold values from -6 to 6
- projection: bfloat16 [1536, 3072], P('fsdp'), may hold values from -1 to 1
- lengths: int32 [16], P(('dp', 'fsdp')), may hold values from 512 to 2048
- cotangent: bfloat16 [16, 2048, 1024], P(('dp', 'fsdp'), 'seq'), may hold values from -24 to 24
Outputs:
- context: bfloat16 [16, 2048, 1024], P(('dp', 'fsdp'), 'seq')
- input_gradient: float32 [16, 2048, 1536], P(('dp', 'fsdp'), 'seq')
- projection_gradient: float32 [1536, 3072], P(('dp', 'fsdp', 'seq'))
All inputs are finite; a program needn't handle non-finite values.
Results may differ from a plain program's by a relative error of at most 0.007.
The roundings to bfloat16 on the way count: a program that leaves them out, or rounds other values in their place, can miss the bound.
Values may be sent and summed in bfloat16 or wider, within the bound.
No kernel may reach another device: no remote copies, remote signals or barrier semaphores. Data moves between devices by JAX's collectives and lax.ppermute only.
A program may use at most 128 MiB of HBM per device.

v0:
```python
import math
import jax
import jax.numpy as jnp
from jax import lax
from jax.sharding import PartitionSpec as P

HEADS = 16
HD = 64
EPS = 1e-05


def block_probabilities(query_block, key_rows, valid):
    factor = 1.0 / math.sqrt(query_block.shape[-1])
    scores = (
        jnp.einsum("qhd,khd->hqk", query_block, key_rows, preferred_element_type=jnp.float32)
        * factor
    )
    scores = jnp.where(valid[None, None, :], scores, -jnp.inf)
    row_peak = jnp.max(scores, axis=2, keepdims=True)
    exponentials = jnp.exp(scores - row_peak)
    return exponentials / jnp.sum(exponentials, axis=2, keepdims=True)


def forward_heads(query_rows, key_rows, value_rows, valid, block_rows):
    total_rows = query_rows.shape[0]

    def forward_one_block(block_index):
        first_row = block_index * block_rows
        query_block = lax.dynamic_slice_in_dim(query_rows, first_row, block_rows, 0)
        probabilities = block_probabilities(query_block, key_rows, valid)
        mixture = jnp.einsum(
            "hqk,khd->qhd",
            probabilities.astype(jnp.bfloat16),
            value_rows,
            preferred_element_type=jnp.float32,
        )
        keep_rows = lax.dynamic_slice_in_dim(valid, first_row, block_rows, 0)
        return jnp.where(keep_rows[:, None, None], mixture, jnp.zeros_like(mixture)).astype(
            jnp.bfloat16
        )

    blocks = lax.map(forward_one_block, jnp.arange(total_rows // block_rows, dtype=jnp.int32))
    return blocks.reshape(query_rows.shape)


def backward_heads(query_rows, key_rows, value_rows, upstream, valid, block_rows):
    total_rows = query_rows.shape[0]
    factor = 1.0 / math.sqrt(query_rows.shape[-1])

    def backward_one_block(running, block_index):
        key_sum, value_sum = running
        first_row = block_index * block_rows
        query_block = lax.dynamic_slice_in_dim(query_rows, first_row, block_rows, 0)
        upstream_block = lax.dynamic_slice_in_dim(upstream, first_row, block_rows, 0)
        keep_rows = lax.dynamic_slice_in_dim(valid, first_row, block_rows, 0)
        upstream_block = jnp.where(
            keep_rows[:, None, None], upstream_block, jnp.zeros_like(upstream_block)
        )
        probabilities = block_probabilities(query_block, key_rows, valid)
        value_sum = value_sum + jnp.einsum(
            "hqk,qhd->khd",
            probabilities.astype(jnp.bfloat16),
            upstream_block,
            preferred_element_type=jnp.float32,
        )
        prob_gradient = jnp.einsum(
            "qhd,khd->hqk", upstream_block, value_rows, preferred_element_type=jnp.float32
        )
        row_inner = jnp.sum(probabilities * prob_gradient, axis=2, keepdims=True)
        score_gradient = (probabilities * (prob_gradient - row_inner) * factor).astype(jnp.bfloat16)
        query_gradient = jnp.einsum(
            "hqk,khd->qhd", score_gradient, key_rows, preferred_element_type=jnp.float32
        ).astype(jnp.bfloat16)
        key_sum = key_sum + jnp.einsum(
            "hqk,qhd->khd", score_gradient, query_block, preferred_element_type=jnp.float32
        )
        return ((key_sum, value_sum), query_gradient)

    empty_sum = jnp.zeros(key_rows.shape, jnp.float32)
    sums, query_blocks = lax.scan(
        backward_one_block,
        (empty_sum, empty_sum),
        jnp.arange(total_rows // block_rows, dtype=jnp.int32),
    )
    return (
        query_blocks.reshape(query_rows.shape),
        sums[0].astype(jnp.bfloat16),
        sums[1].astype(jnp.bfloat16),
    )


def body(frames, projection, lengths, cotangent):
    inputs = frames[0]
    upstream = cotangent[0]
    length = lengths[0]
    seq_count = lax.axis_size("seq")
    local_rows, feature_count = inputs.shape
    total_rows = local_rows * seq_count
    head_count = HEADS // seq_count
    group_width = head_count * HD
    block_rows = 512
    as_float = inputs.astype(jnp.float32)
    centered = as_float - jnp.mean(as_float, axis=1, keepdims=True)
    inv_std = lax.rsqrt(jnp.mean(centered * centered, axis=1, keepdims=True) + EPS)
    standard = centered * inv_std
    normed = standard.astype(jnp.bfloat16)
    valid = jnp.arange(total_rows, dtype=jnp.int32) < length
    weight_full = lax.all_gather(projection, "fsdp", axis=0, tiled=True)
    packed = jnp.dot(normed, weight_full, preferred_element_type=jnp.float32).astype(jnp.bfloat16)
    packed = packed.reshape(local_rows, 3, seq_count, group_width)
    upstream_four = upstream.reshape(local_rows, 1, seq_count, group_width)
    head_inputs, head_upstream = (
        lax.all_to_all(packed, "seq", split_axis=2, concat_axis=0, tiled=True),
        lax.all_to_all(upstream_four, "seq", split_axis=2, concat_axis=0, tiled=True),
    )
    head_inputs = head_inputs.reshape(total_rows, 3, head_count, HD)
    head_grads = head_upstream.reshape(total_rows, head_count, HD)
    query_rows = head_inputs[:, 0]
    key_rows = head_inputs[:, 1]
    value_rows = head_inputs[:, 2]
    mixture = forward_heads(query_rows, key_rows, value_rows, valid, block_rows)
    returned_context = lax.all_to_all(
        mixture.reshape(total_rows, 1, group_width), "seq", split_axis=0, concat_axis=1, tiled=True
    )
    context = returned_context.reshape(local_rows, seq_count * group_width)
    query_gradient, key_gradient, value_gradient = backward_heads(
        query_rows, key_rows, value_rows, head_grads, valid, block_rows
    )
    stacked = jnp.stack([query_gradient, key_gradient, value_gradient], axis=1).reshape(
        total_rows, 3, 1, group_width
    )
    returned = lax.all_to_all(stacked, "seq", split_axis=0, concat_axis=2, tiled=True)
    packed_gradient = returned.reshape(local_rows, 3 * seq_count * group_width)
    normed_gradient = lax.dot_general(
        packed_gradient, weight_full, (((1,), (1,)), ((), ())), preferred_element_type=jnp.float32
    )
    projection_gradient = lax.psum_scatter(
        lax.dot_general(
            normed, packed_gradient, (((0,), (0,)), ((), ())), preferred_element_type=jnp.float32
        ),
        ("dp", "fsdp", "seq"),
        scatter_dimension=0,
        tiled=True,
    )
    row_mean = jnp.mean(normed_gradient, axis=1, keepdims=True)
    projected = jnp.mean(normed_gradient * standard, axis=1, keepdims=True)
    input_gradient = inv_std * (normed_gradient - row_mean - standard * projected)
    return (context[None], input_gradient[None], projection_gradient)


def solution(mesh):
    placed = (
        P(("dp", "fsdp"), "seq", None),
        P("fsdp", None),
        P(("dp", "fsdp")),
        P(("dp", "fsdp"), "seq", None),
    )
    return jax.shard_map(
        body,
        mesh=mesh,
        in_specs=placed,
        out_specs=(
            P(("dp", "fsdp"), "seq", None),
            P(("dp", "fsdp"), "seq", None),
            P(("dp", "fsdp", "seq"), None),
        ),
        check_vma=False,
    )
```

profile of v0, /device:TPU:2, one launch (start us, length us, event | category | flops | bytes accessed | tf_op | source)
XLA Modules:
  0.0 1038.3 jit_solution(2263338651254375848)
XLA Ops:
  9.9 5.8 all-to-all-start.2
  18.6 61.9 %all-gather.2.cloned.1.call-done = bf16[1536,3072]{1,0:T(8,128)(2,1)} async-done(((bf16[384,3072]{1,0:T(8,128)(2,1)}), bf16[1536,3072]{1,0:T(8,128)(2,1)}) %all-gather.2.cloned.1.call-update) | async-done | bytes 9437200 | tf_op jit(solution)/shard_map/all_gather | solution.py:108
  80.5 6.7 fusion.105
  89.0 4.4 all-to-all-start
  94.6 20.5 %all-to-all-done = bf16[256,3,8,128]{3,0,1,2:T(8,128)(2,1)S(1)} async-done(((bf16[256,3,8,128]{3,0,1,2:T(8,128)(2,1)}), bf16[256,3,8,128]{3,0,1,2:T(8,128)(2,1)S(1)}, u32[]{:S(2)}, u32[]{:S(2)}) %all-to-all-start) | async-done | bytes 1572896 | tf_op jit(solution)/shard_map/all_to_all | solution.py:113
  116.9 2.6 reshape.79
  120.5 197.0 %while.26 = (s32[]{:T(128)}, f32[2048,2,64]{0,2,1:T(8,128)}, f32[2048,2,64]{0,2,1:T(8,128)}, bf16[4,512,2,64]{1,3,2,0:T(8,128)(2,1)S(1)}, s32[4]{0:T(128)S(1)}, ...) while((s32[]{:T(128)}, f32[2048,2,64]{0,2,1:T(8,128)}, ...), condition=%wide.region_10.11_spmd.clone, body=%wide.region_6.10_spmd.clone.sunk | while | flops 1385373696 | bytes 107115288 | solution.py:80
  121.8 4.6 fusion.167
  126.4 6.6 fusion.168
  132.9 14.4 %fusion.171 = bf16[4,512,2,64]{1,3,2,0:T(8,128)(2,1)S(1)} fusion(bf16[4,512,2,64]{1,3,2,0:T(8,128)(2,1)S(1)} %get-tuple-element.351, s32[]{:T(128)} %get-tuple-element.348, bf16[2048,2,64]{0,2,1:T(8,128)(2,1)S(1)} %get-tuple-element.369, f32[2,512,2048]{2,1,0:T(8,128)} %fusion.167, f32[2,512,2048]{2,1,0:T(8,128)} %get-tuple-element.299, ...), kind=kOutput, calls=%fused_computation.43.clone.1 | convolution fusion | flops 283184128 | bytes 34218496 | tf_op jit(solution)/shard_map/while/body/eval_jaxpr/hqk,khd->qhd/dot_general | solution.py:71
  147.4 5.4 fusion.170
  152.8 15.8 %fusion.169 = f32[2048,2,64]{0,2,1:T(8,128)S(1)} fusion(f32[2,512,2048]{2,1,0:T(8,128)} %fusion.167, f32[2048,2,64]{0,2,1:T(8,128)S(1)} %copy-done.1, pred[]{:T(512)S(6)} %compare.3, bf16[2048,2,64]{0,2,1:T(8,128)(2,1)} %get-tuple-element.367, s32[]{:T(128)S(6)} %select_n.71, f32[2,512,2048]{2,1,0:T(8,128)} %get-tuple-element.299, ...), kind=kOutput, calls=%fused_computation.40.clone.1 | convolution fusion | flops 283642880 | bytes 35790852 | tf_op jit(solution)/shard_map/while/body/eval_jaxpr/hqk,qhd->khd/dot_general | solution.py:74
  170.9 4.6 fusion.167
  175.4 6.6 fusion.168
  182.0 14.4 %fusion.171 = bf16[4,512,2,64]{1,3,2,0:T(8,128)(2,1)S(1)} fusion(bf16[4,512,2,64]{1,3,2,0:T(8,128)(2,1)S(1)} %get-tuple-element.351, s32[]{:T(128)} %get-tuple-element.348, bf16[2048,2,64]{0,2,1:T(8,128)(2,1)S(1)} %get-tuple-element.369, f32[2,512,2048]{2,1,0:T(8,128)} %fusion.167, f32[2,512,2048]{2,1,0:T(8,128)} %get-tuple-element.299, ...), kind=kOutput, calls=%fused_computation.43.clone.1 | convolution fusion | flops 283184128 | bytes 34218496 | tf_op jit(solution)/shard_map/while/body/eval_jaxpr/hqk,khd->qhd/dot_general | solution.py:71
  196.4 5.6 fusion.170
  202.1 15.8 %fusion.169 = f32[2048,2,64]{0,2,1:T(8,128)S(1)} fusion(f32[2,512,2048]{2,1,0:T(8,128)} %fusion.167, f32[2048,2,64]{0,2,1:T(8,128)S(1)} %copy-done.1, pred[]{:T(512)S(6)} %compare.3, bf16[2048,2,64]{0,2,1:T(8,128)(2,1)} %get-tuple-element.367, s32[]{:T(128)S(6)} %select_n.71, f32[2,512,2048]{2,1,0:T(8,128)} %get-tuple-element.299, ...), kind=kOutput, calls=%fused_computation.40.clone.1 | convolution fusion | flops 283642880 | bytes 35790852 | tf_op jit(solution)/shard_map/while/body/eval_jaxpr/hqk,qhd->khd/dot_general | solution.py:74
  220.2 4.6 fusion.167
  224.8 6.6 fusion.168
  231.3 14.4 %fusion.171 = bf16[4,512,2,64]{1,3,2,0:T(8,128)(2,1)S(1)} fusion(bf16[4,512,2,64]{1,3,2,0:T(8,128)(2,1)S(1)} %get-tuple-element.351, s32[]{:T(128)} %get-tuple-element.348, bf16[2048,2,64]{0,2,1:T(8,128)(2,1)S(1)} %get-tuple-element.369, f32[2,512,2048]{2,1,0:T(8,128)} %fusion.167, f32[2,512,2048]{2,1,0:T(8,128)} %get-tuple-element.299, ...), kind=kOutput, calls=%fused_computation.43.clone.1 | convolution fusion | flops 283184128 | bytes 34218496 | tf_op jit(solution)/shard_map/while/body/eval_jaxpr/hqk,khd->qhd/dot_general | solution.py:71
  245.7 5.6 fusion.170
  251.4 15.8 %fusion.169 = f32[2048,2,64]{0,2,1:T(8,128)S(1)} fusion(f32[2,512,2048]{2,1,0:T(8,128)} %fusion.167, f32[2048,2,64]{0,2,1:T(8,128)S(1)} %copy-done.1, pred[]{:T(512)S(6)} %compare.3, bf16[2048,2,64]{0,2,1:T(8,128)(2,1)} %get-tuple-element.367, s32[]{:T(128)S(6)} %select_n.71, f32[2,512,2048]{2,1,0:T(8,128)} %get-tuple-element.299, ...), kind=kOutput, calls=%fused_computation.40.clone.1 | convolution fusion | flops 283642880 | bytes 35790852 | tf_op jit(solution)/shard_map/while/body/eval_jaxpr/hqk,qhd->khd/dot_general | solution.py:74
  269.5 4.6 fusion.167
  274.1 6.6 fusion.168
  280.7 14.4 %fusion.171 = bf16[4,512,2,64]{1,3,2,0:T(8,128)(2,1)S(1)} fusion(bf16[4,512,2,64]{1,3,2,0:T(8,128)(2,1)S(1)} %get-tuple-element.351, s32[]{:T(128)} %get-tuple-element.348, bf16[2048,2,64]{0,2,1:T(8,128)(2,1)S(1)} %get-tuple-element.369, f32[2,512,2048]{2,1,0:T(8,128)} %fusion.167, f32[2,512,2048]{2,1,0:T(8,128)} %get-tuple-element.299, ...), kind=kOutput, calls=%fused_computation.43.clone.1 | convolution fusion | flops 283184128 | bytes 34218496 | tf_op jit(solution)/shard_map/while/body/eval_jaxpr/hqk,khd->qhd/dot_general | solution.py:71
  295.1 5.6 fusion.170
  300.7 15.8 %fusion.169 = f32[2048,2,64]{0,2,1:T(8,128)S(1)} fusion(f32[2,512,2048]{2,1,0:T(8,128)} %fusion.167, f32[2048,2,64]{0,2,1:T(8,128)S(1)} %copy-done.1, pred[]{:T(512)S(6)} %compare.3, bf16[2048,2,64]{0,2,1:T(8,128)(2,1)} %get-tuple-element.367, s32[]{:T(128)S(6)} %select_n.71, f32[2,512,2048]{2,1,0:T(8,128)} %get-tuple-element.299, ...), kind=kOutput, calls=%fused_computation.40.clone.1 | convolution fusion | flops 283642880 | bytes 35790852 | tf_op jit(solution)/shard_map/while/body/eval_jaxpr/hqk,qhd->khd/dot_general | solution.py:74
  322.2 3.0 copy.54
  325.3 30.3 %all_to_all.60 = bf16[2048,3,1,128]{3,1,2,0:T(4,128)(2,1)S(1)} all-to-all(bf16[2048,3,1,128]{3,1,2,0:T(4,128)(2,1)S(1)} %copy.54), channel_id=1, replica_groups=mesh['dp'=4,'fsdp'=4,'seq'=8] {'seq'}, dimensions={0} | all-to-all | bytes 3145728 | tf_op jit(solution)/shard_map/all_to_all | solution.py:132
  358.7 8.0 fusion.107
  366.7 325.4 %fusion = f32[16,3072]{1,0:T(8,128)} fusion(f32[1536,3072]{1,0:T(8,128)} %fusion.107), kind=kCustom, calls=%all-reduce-scatter | all-reduce-scatter fusion | flops 6291457 | bytes 19070976
  692.2 3.4 collective-permute-start
  696.6 4.1 collective-permute-start.31
  704.5 6.7 collective-permute-start.11
  711.2 33.2 %collective-permute-done.31 = f32[12,3072]{1,0:T(8,128)S(1)} collective-permute-done((f32[12,3072]{1,0:T(8,128)S(1)}, f32[12,3072]{1,0:T(8,128)S(1)}, u32[]{:S(2)}, u32[]{:S(2)}) %collective-permute-start.31) | collective-permute-done | bytes 147488
  748.4 51.9 %while.25 = (s32[]{:T(128)}, bf16[4,512,2,64]{1,3,2,0:T(8,128)(2,1)S(1)}, s32[4]{0:T(128)S(1)}, pred[2048]{0:T(1024)(128)(4,1)S(1)}, bf16[2048,2,64]{0,2,1:T(8,1...) while((s32[]{:T(128)}, ...), condition=%wide.region_5.6_spmd, body=%wide.region_2.5_spmd.sunk | while | flops 549586944 | bytes 18099892 | solution.py:42
  749.6 6.9 fusion.157
  756.5 4.8 fusion.158
  762.5 6.9 fusion.157
  769.5 4.8 fusion.158
  775.5 6.9 fusion.157
  782.4 4.8 fusion.158
  788.5 6.9 fusion.157
  795.4 4.8 fusion.158
  802.2 5.0 reshape.82
  807.7 12.6 %reduce.1 = bf16[2048,128]{1,0:T(8,128)(2,1)S(1)} reduce(bf16[2048,1,128]{2,1,0:T(2,128)(2,1)} %reshape.82, bf16[]{:T(256)} %broadcast.123), dimensions={1}, to_apply=%reshape.82.reduce_sub_computation | reduce | bytes 1048578 | tf_op jit(solution)/shard_map/reshape;reshape | solution.py:123
  821.2 3.5 all-to-all-start.1
  824.7 13.4 %collective-permute-start.14 = (f32[16,3072]{1,0:T(8,128)}, f32[16,3072]{1,0:T(8,128)}, u32[]{:S(2)}, u32[]{:S(2)}) collective-permute-start(f32[16,3072]{1,0:T(8,128)} %fusion), channel_id=1, source_target_pairs={{0,15},{1,16},{2,17},{3,18},{4,19},{5,20},{6,21},{7,22},{8,23},{9,... | collective-permute-start | bytes 589832
  840.1 3.9 collective-permute-start.16
  844.0 4.9 collective-permute-start.17
  848.9 2.2 collective-permute-start.18
  853.1 9.9 collective-permute-start.2
  863.1 5.8 collective-permute-start.20
  868.9 5.6 collective-permute-start.21
  884.8 5.5 collective-permute-start.25
  894.4 5.5 fusion.114
  903.8 2.8 collective-permute-start.3
  911.0 2.3 collective-permute-done.28
  913.3 6.2 collective-permute-start.5
  919.5 4.9 collective-permute-start.6
  924.4 3.9 collective-permute-start.7
  930.3 5.6 collective-permute-start.9
  937.5 6.3 collective-permute-done.8
  945.8 84.0 %concatenate.1 = f32[524,3072]{1,0:T(8,128)} concatenate(f32[12,3072]{1,0:T(8,128)S(1)} %copy-done.7, f32[16,3072]{1,0:T(8,128)S(1)} %collective-permute-done.30, f32[16,3072]{1,0:T(8,128)S(1)} %collective-permute-done.29, f32[16,3072]{1,0:T(8,128)S(1)} %collective-permute-done.28, f32[16,3072]{1,0:T(8,128)} %copy-done.9, f32[16,3072]{1,0:T(8,128)} %copy-done.8, ...), dimensions={0} | concatenate | bytes 12877824
  (141 shorter events, 73.5 us)
Async XLA Ops:
  7.2 73.3 %all-gather.2.cloned.1.call-start = ((), (), s32[]{:S(2)}) async-start(), calls=%async_computation.4 | async-start | bytes 11796480 | tf_op jit(solution)/shard_map/all_gather | solution.py:108
  9.9 79.0 %all-to-all-start.2 = ((bf16[256,1,8,128]{0,3,1,2:T(8,128)(2,1)}), bf16[256,1,8,128]{0,3,1,2:T(8,128)(2,1)S(1)}, u32[]{:S(2)}, u32[]{:S(2)}) async-start(bf16[256,1,8,128]{0,3,1,2:T(8,128)(2,1)} %bitcast.12), calls=%async_computation.2 | async-start | bytes 1048576 | tf_op jit(solution)/shard_map/all_to_all | solution.py:114
  17.1 70.1 %copy-start.10 = (f32[256]{0:T(256)}, f32[256]{0:T(256)S(1)}, u32[]{:S(2)}) copy-start(f32[256]{0:T(256)S(1)} %broadcast_multiply_fusion.2) | copy-start | bytes 3076
  18.6 68.6 %copy-start.12 = (f32[256]{0:T(256)}, f32[256]{0:T(256)S(1)}, u32[]{:S(2)}) copy-start(f32[256]{0:T(256)S(1)} %add_rsqrt_fusion) | copy-start | bytes 3076
  89.0 26.1 %all-to-all-start = ((bf16[256,3,8,128]{3,0,1,2:T(8,128)(2,1)}), bf16[256,3,8,128]{3,0,1,2:T(8,128)(2,1)S(1)}, u32[]{:S(2)}, u32[]{:S(2)}) async-start(bf16[256,3,8,128]{3,0,1,2:T(8,128)(2,1)} %copy.46), calls=%async_computation | async-start | bytes 3145728 | tf_op jit(solution)/shard_map/all_to_all | solution.py:113
  147.3 5.4 copy-start.1
  168.5 1.0 copy-start.2
  196.4 5.7 copy-start.1
  217.9 1.0 copy-start.2
  245.7 5.6 copy-start.1
  267.2 1.0 copy-start.2
  295.1 5.7 copy-start.1
  316.5 1.0 copy-start.2
  317.5 3.4 copy-start.3
  320.9 37.8 %copy-start = (bf16[1,256,1536]{2,1,0:T(8,128)(2,1)S(1)}, bf16[1,256,1536]{2,1,0:T(8,128)(2,1)}, u32[]{:S(2)}) copy-start(bf16[1,256,1536]{2,1,0:T(8,128)(2,1)} %param.8) | copy-start | bytes 2359300
  320.9 37.8 %copy-start.11 = (f32[256]{0:T(256)S(1)}, f32[256]{0:T(256)}, u32[]{:S(2)}) copy-start(f32[256]{0:T(256)} %copy-done.10) | copy-start | bytes 3076
  320.9 37.8 %copy-start.13 = (f32[256]{0:T(256)S(1)}, f32[256]{0:T(256)}, u32[]{:S(2)}) copy-start(f32[256]{0:T(256)} %copy-done.12) | copy-start | bytes 3076
  692.2 54.2 %collective-permute-start = (f32[16,3072]{1,0:T(8,128)}, f32[16,3072]{1,0:T(8,128)S(1)}, u32[]{:S(2)}, u32[]{:S(2)}) collective-permute-start(f32[16,3072]{1,0:T(8,128)} %fusion), channel_id=1, source_target_pairs={{0,1},{1,2},{2,3},{3,4},{4,5},{5,6},{6,7},{7,8},{8,9},{9,10},{10,1... | collective-permute-start | bytes 589832
  696.6 47.9 %collective-permute-start.31 = (f32[12,3072]{1,0:T(8,128)S(1)}, f32[12,3072]{1,0:T(8,128)S(1)}, u32[]{:S(2)}, u32[]{:S(2)}) collective-permute-start(f32[12,3072]{1,0:T(8,128)S(1)} %slice.15), channel_id=1, source_target_pairs={{0,32},{1,33},{2,34},{3,35},{4,36},{5,37},{6,38},{7,39},{8,40},{9,... | collective-permute-start | bytes 442376
  700.6 124.1 %collective-permute-start.1 = (f32[16,3072]{1,0:T(8,128)}, f32[16,3072]{1,0:T(8,128)}, u32[]{:S(2)}, u32[]{:S(2)}) collective-permute-start(f32[16,3072]{1,0:T(8,128)} %fusion), channel_id=1, source_target_pairs={{0,2},{1,3},{2,4},{3,5},{4,6},{5,7},{6,8},{7,9},{8,10},{9,11},{10,... | collective-permute-start | bytes 589832
  702.6 135.5 %collective-permute-start.10 = (f32[16,3072]{1,0:T(8,128)}, f32[16,3072]{1,0:T(8,128)}, u32[]{:S(2)}, u32[]{:S(2)}) collective-permute-start(f32[16,3072]{1,0:T(8,128)} %fusion), channel_id=1, source_target_pairs={{0,11},{1,12},{2,13},{3,14},{4,15},{5,16},{6,17},{7,18},{8,19},{9,... | collective-permute-start | bytes 589832
  704.5 135.6 %collective-permute-start.11 = (f32[16,3072]{1,0:T(8,128)}, f32[16,3072]{1,0:T(8,128)}, u32[]{:S(2)}, u32[]{:S(2)}) collective-permute-start(f32[16,3072]{1,0:T(8,128)} %fusion), channel_id=1, source_target_pairs={{0,12},{1,13},{2,14},{3,15},{4,16},{5,17},{6,18},{7,19},{8,20},{9,... | collective-permute-start | bytes 589832
  744.4 3.9 copy-start.6
  744.4 99.6 %collective-permute-start.12 = (f32[16,3072]{1,0:T(8,128)}, f32[16,3072]{1,0:T(8,128)}, u32[]{:S(2)}, u32[]{:S(2)}) collective-permute-start(f32[16,3072]{1,0:T(8,128)} %fusion), channel_id=1, source_target_pairs={{0,13},{1,14},{2,15},{3,16},{4,17},{5,18},{6,19},{7,20},{8,21},{9,... | collective-permute-start | bytes 589832
  746.4 2.0 copy-start.4
  746.4 102.5 %collective-permute-start.13 = (f32[16,3072]{1,0:T(8,128)}, f32[16,3072]{1,0:T(8,128)}, u32[]{:S(2)}, u32[]{:S(2)}) collective-permute-start(f32[16,3072]{1,0:T(8,128)} %fusion), channel_id=1, source_target_pairs={{0,14},{1,15},{2,16},{3,17},{4,18},{5,19},{6,20},{7,21},{8,22},{9,... | collective-permute-start | bytes 589832
  821.2 55.2 %all-to-all-start.1 = ((bf16[8,2,16384]{2,1,0:T(2,128)(2,1)}), bf16[8,2,16384]{2,1,0:T(2,128)(2,1)S(1)}, u32[]{:S(2)}, u32[]{:S(2)}) async-start(bf16[8,2,16384]{2,1,0:T(2,128)(2,1)} %reshape.83), calls=%async_computation.1 | async-start | bytes 1048576 | tf_op jit(solution)/shard_map/all_to_all | solution.py:122
  824.7 26.4 %collective-permute-start.14 = (f32[16,3072]{1,0:T(8,128)}, f32[16,3072]{1,0:T(8,128)}, u32[]{:S(2)}, u32[]{:S(2)}) collective-permute-start(f32[16,3072]{1,0:T(8,128)} %fusion), channel_id=1, source_target_pairs={{0,15},{1,16},{2,17},{3,18},{4,19},{5,20},{6,21},{7,22},{8,23},{9,... | collective-permute-start | bytes 589832
  838.1 15.0 %collective-permute-start.15 = (f32[16,3072]{1,0:T(8,128)}, f32[16,3072]{1,0:T(8,128)}, u32[]{:S(2)}, u32[]{:S(2)}) collective-permute-start(f32[16,3072]{1,0:T(8,128)} %fusion), channel_id=1, source_target_pairs={{0,16},{1,17},{2,18},{3,19},{4,20},{5,21},{6,22},{7,23},{8,24},{9,... | collective-permute-start | bytes 589832
  840.1 23.0 %collective-permute-start.16 = (f32[16,3072]{1,0:T(8,128)}, f32[16,3072]{1,0:T(8,128)}, u32[]{:S(2)}, u32[]{:S(2)}) collective-permute-start(f32[16,3072]{1,0:T(8,128)} %fusion), channel_id=1, source_target_pairs={{0,17},{1,18},{2,19},{3,20},{4,21},{5,22},{6,23},{7,24},{8,25},{9,... | collective-permute-start | bytes 589832
  844.0 24.8 %collective-permute-start.17 = (f32[16,3072]{1,0:T(8,128)}, f32[16,3072]{1,0:T(8,128)}, u32[]{:S(2)}, u32[]{:S(2)}) collective-permute-start(f32[16,3072]{1,0:T(8,128)} %fusion), channel_id=1, source_target_pairs={{0,18},{1,19},{2,20},{3,21},{4,22},{5,23},{6,24},{7,25},{8,26},{9,... | collective-permute-start | bytes 589832
  848.9 25.6 %collective-permute-start.18 = (f32[16,3072]{1,0:T(8,128)}, f32[16,3072]{1,0:T(8,128)}, u32[]{:S(2)}, u32[]{:S(2)}) collective-permute-start(f32[16,3072]{1,0:T(8,128)} %fusion), channel_id=1, source_target_pairs={{0,19},{1,20},{2,21},{3,22},{4,23},{5,24},{6,25},{7,26},{8,27},{9,... | collective-permute-start | bytes 589832
  851.2 29.6 %collective-permute-start.19 = (f32[16,3072]{1,0:T(8,128)}, f32[16,3072]{1,0:T(8,128)}, u32[]{:S(2)}, u32[]{:S(2)}) collective-permute-start(f32[16,3072]{1,0:T(8,128)} %fusion), channel_id=1, source_target_pairs={{0,20},{1,21},{2,22},{3,23},{4,24},{5,25},{6,26},{7,27},{8,28},{9,... | collective-permute-start | bytes 589832
  853.1 29.7 %collective-permute-start.2 = (f32[16,3072]{1,0:T(8,128)}, f32[16,3072]{1,0:T(8,128)}, u32[]{:S(2)}, u32[]{:S(2)}) collective-permute-start(f32[16,3072]{1,0:T(8,128)} %fusion), channel_id=1, source_target_pairs={{0,3},{1,4},{2,5},{3,6},{4,7},{5,8},{6,9},{7,10},{8,11},{9,12},{10... | collective-permute-start | bytes 589832
  863.1 21.7 %collective-permute-start.20 = (f32[16,3072]{1,0:T(8,128)}, f32[16,3072]{1,0:T(8,128)}, u32[]{:S(2)}, u32[]{:S(2)}) collective-permute-start(f32[16,3072]{1,0:T(8,128)} %fusion), channel_id=1, source_target_pairs={{0,21},{1,22},{2,23},{3,24},{4,25},{5,26},{6,27},{7,28},{8,29},{9,... | collective-permute-start | bytes 589832
  868.9 21.4 %collective-permute-start.21 = (f32[16,3072]{1,0:T(8,128)}, f32[16,3072]{1,0:T(8,128)}, u32[]{:S(2)}, u32[]{:S(2)}) collective-permute-start(f32[16,3072]{1,0:T(8,128)} %fusion), channel_id=1, source_target_pairs={{0,22},{1,23},{2,24},{3,25},{4,26},{5,27},{6,28},{7,29},{8,30},{9,... | collective-permute-start | bytes 589832
  874.5 17.7 %collective-permute-start.22 = (f32[16,3072]{1,0:T(8,128)}, f32[16,3072]{1,0:T(8,128)}, u32[]{:S(2)}, u32[]{:S(2)}) collective-permute-start(f32[16,3072]{1,0:T(8,128)} %fusion), channel_id=1, source_target_pairs={{0,23},{1,24},{2,25},{3,26},{4,27},{5,28},{6,29},{7,30},{8,31},{9,... | collective-permute-start | bytes 589832
  880.8 65.0 %copy-start.5 = (f32[16,3072]{1,0:T(8,128)S(1)}, f32[16,3072]{1,0:T(8,128)}, u32[]{:S(2)}) copy-start(f32[16,3072]{1,0:T(8,128)} %copy-done.4) | copy-start | bytes 589828
  880.8 65.0 %copy-start.7 = (f32[12,3072]{1,0:T(8,128)S(1)}, f32[12,3072]{1,0:T(8,128)}, u32[]{:S(2)}) copy-start(f32[12,3072]{1,0:T(8,128)} %copy-done.6) | copy-start | bytes 442372
  880.8 19.2 %collective-permute-start.23 = (f32[16,3072]{1,0:T(8,128)}, f32[16,3072]{1,0:T(8,128)S(1)}, u32[]{:S(2)}, u32[]{:S(2)}) collective-permute-start(f32[16,3072]{1,0:T(8,128)} %fusion), channel_id=1, source_target_pairs={{0,24},{1,25},{2,26},{3,27},{4,28},{5,29},{6,30},{7,31},{8,32},{9,... | collective-permute-start | bytes 589832
  882.8 19.1 %collective-permute-start.24 = (f32[16,3072]{1,0:T(8,128)}, f32[16,3072]{1,0:T(8,128)S(1)}, u32[]{:S(2)}, u32[]{:S(2)}) collective-permute-start(f32[16,3072]{1,0:T(8,128)} %fusion), channel_id=1, source_target_pairs={{0,25},{1,26},{2,27},{3,28},{4,29},{5,30},{6,31},{7,32},{8,33},{9,... | collective-permute-start | bytes 589832
  884.8 19.1 %collective-permute-start.25 = (f32[16,3072]{1,0:T(8,128)}, f32[16,3072]{1,0:T(8,128)S(1)}, u32[]{:S(2)}, u32[]{:S(2)}) collective-permute-start(f32[16,3072]{1,0:T(8,128)} %fusion), channel_id=1, source_target_pairs={{0,26},{1,27},{2,28},{3,29},{4,30},{5,31},{6,32},{7,33},{8,34},{9,... | collective-permute-start | bytes 589832
  890.3 16.6 %collective-permute-start.26 = (f32[16,3072]{1,0:T(8,128)}, f32[16,3072]{1,0:T(8,128)S(1)}, u32[]{:S(2)}, u32[]{:S(2)}) collective-permute-start(f32[16,3072]{1,0:T(8,128)} %fusion), channel_id=1, source_target_pairs={{0,27},{1,28},{2,29},{3,30},{4,31},{5,32},{6,33},{7,34},{8,35},{9,... | collective-permute-start | bytes 589832
  892.2 16.6 %collective-permute-start.27 = (f32[16,3072]{1,0:T(8,128)}, f32[16,3072]{1,0:T(8,128)S(1)}, u32[]{:S(2)}, u32[]{:S(2)}) collective-permute-start(f32[16,3072]{1,0:T(8,128)} %fusion), channel_id=1, source_target_pairs={{0,28},{1,29},{2,30},{3,31},{4,32},{5,33},{6,34},{7,35},{8,36},{9,... | collective-permute-start | bytes 589832
  900.0 13.4 %collective-permute-start.28 = (f32[16,3072]{1,0:T(8,128)}, f32[16,3072]{1,0:T(8,128)S(1)}, u32[]{:S(2)}, u32[]{:S(2)}) collective-permute-start(f32[16,3072]{1,0:T(8,128)} %fusion), channel_id=1, source_target_pairs={{0,29},{1,30},{2,31},{3,32},{4,33},{5,34},{6,35},{7,36},{8,37},{9,... | collective-permute-start | bytes 589832
  901.9 17.6 %collective-permute-start.29 = (f32[16,3072]{1,0:T(8,128)}, f32[16,3072]{1,0:T(8,128)S(1)}, u32[]{:S(2)}, u32[]{:S(2)}) collective-permute-start(f32[16,3072]{1,0:T(8,128)} %fusion), channel_id=1, source_target_pairs={{0,30},{1,31},{2,32},{3,33},{4,34},{5,35},{6,36},{7,37},{8,38},{9,... | collective-permute-start | bytes 589832
  903.8 20.6 %collective-permute-start.3 = (f32[16,3072]{1,0:T(8,128)}, f32[16,3072]{1,0:T(8,128)S(1)}, u32[]{:S(2)}, u32[]{:S(2)}) collective-permute-start(f32[16,3072]{1,0:T(8,128)} %fusion), channel_id=1, source_target_pairs={{0,4},{1,5},{2,6},{3,7},{4,8},{5,9},{6,10},{7,11},{8,12},{9,13},{1... | collective-permute-start | bytes 589832
  906.9 30.6 %copy-start.8 = (f32[16,3072]{1,0:T(8,128)}, f32[16,3072]{1,0:T(8,128)S(1)}, u32[]{:S(2)}) copy-start(f32[16,3072]{1,0:T(8,128)S(1)} %collective-permute-done.26) | copy-start | bytes 589828
  906.9 21.4 %collective-permute-start.30 = (f32[16,3072]{1,0:T(8,128)}, f32[16,3072]{1,0:T(8,128)S(1)}, u32[]{:S(2)}, u32[]{:S(2)}) collective-permute-start(f32[16,3072]{1,0:T(8,128)} %fusion), channel_id=1, source_target_pairs={{0,31},{1,32},{2,33},{3,34},{4,35},{5,36},{6,37},{7,38},{8,39},{9,... | collective-permute-start | bytes 589832
  908.9 28.6 %copy-start.9 = (f32[16,3072]{1,0:T(8,128)}, f32[16,3072]{1,0:T(8,128)S(1)}, u32[]{:S(2)}) copy-start(f32[16,3072]{1,0:T(8,128)S(1)} %collective-permute-done.27) | copy-start | bytes 589828
  908.9 21.4 %collective-permute-start.4 = (f32[16,3072]{1,0:T(8,128)}, f32[16,3072]{1,0:T(8,128)S(1)}, u32[]{:S(2)}, u32[]{:S(2)}) collective-permute-start(f32[16,3072]{1,0:T(8,128)} %fusion), channel_id=1, source_target_pairs={{0,5},{1,6},{2,7},{3,8},{4,9},{5,10},{6,11},{7,12},{8,13},{9,14},{... | collective-permute-start | bytes 589832
  913.3 24.1 %collective-permute-start.5 = (f32[16,3072]{1,0:T(8,128)}, f32[16,3072]{1,0:T(8,128)S(1)}, u32[]{:S(2)}, u32[]{:S(2)}) collective-permute-start(f32[16,3072]{1,0:T(8,128)} %fusion), channel_id=1, source_target_pairs={{0,6},{1,7},{2,8},{3,9},{4,10},{5,11},{6,12},{7,13},{8,14},{9,15},... | collective-permute-start | bytes 589832
  919.5 18.0 %collective-permute-start.6 = (f32[16,3072]{1,0:T(8,128)}, f32[16,3072]{1,0:T(8,128)S(1)}, u32[]{:S(2)}, u32[]{:S(2)}) collective-permute-start(f32[16,3072]{1,0:T(8,128)} %fusion), channel_id=1, source_target_pairs={{0,7},{1,8},{2,9},{3,10},{4,11},{5,12},{6,13},{7,14},{8,15},{9,16}... | collective-permute-start | bytes 589832
  924.4 13.1 %collective-permute-start.7 = (f32[16,3072]{1,0:T(8,128)}, f32[16,3072]{1,0:T(8,128)S(1)}, u32[]{:S(2)}, u32[]{:S(2)}) collective-permute-start(f32[16,3072]{1,0:T(8,128)} %fusion), channel_id=1, source_target_pairs={{0,8},{1,9},{2,10},{3,11},{4,12},{5,13},{6,14},{7,15},{8,16},{9,17... | collective-permute-start | bytes 589832
  928.3 15.5 %collective-permute-start.8 = (f32[16,3072]{1,0:T(8,128)}, f32[16,3072]{1,0:T(8,128)}, u32[]{:S(2)}, u32[]{:S(2)}) collective-permute-start(f32[16,3072]{1,0:T(8,128)} %fusion), channel_id=1, source_target_pairs={{0,9},{1,10},{2,11},{3,12},{4,13},{5,14},{6,15},{7,16},{8,17},{9,1... | collective-permute-start | bytes 589832
  930.3 15.5 %collective-permute-start.9 = (f32[16,3072]{1,0:T(8,128)}, f32[16,3072]{1,0:T(8,128)}, u32[]{:S(2)}, u32[]{:S(2)}) collective-permute-start(f32[16,3072]{1,0:T(8,128)} %fusion), channel_id=1, source_target_pairs={{0,10},{1,11},{2,12},{3,13},{4,14},{5,15},{6,16},{7,17},{8,18},{9,... | collective-permute-start | bytes 589832
Sparse Core Ops, SparseCore 0:
  9.7 70.7 all-gather.1
where the time goes:
time: 1040 us
  blocking collectives  356 us (34%)
  matrix products  254 us (24%)
  starting transfers between devices  134 us (13%)
  waiting for transfers between devices  127 us (12%)
  local copies, waits for them, and re-layouts  125 us (12%)
  other arithmetic  20.9 us (2%)
  between operations  15.5 us (1%)
    unnamed x1, blocking collectives  325 us
    unnamed x32, starting transfers between devices  120 us
    unnamed x33, local copies, waits for them, and re-layouts  94 us
    dot_general x4, matrix products, backward_one_block(): jnp.einsum('hqk,qhd->khd', score_gradient, query_block, preferred_element...  63.1 us
    all_gather x1, waiting for transfers between devices, body(): weight_full = lax.all_gather(projection, 'fsdp', axis=0, tiled=True)  61.9 us
    dot_general x4, matrix products, backward_one_block(): jnp.einsum('hqk,khd->qhd', score_gradient, key_rows, preferred_element_ty...  57.5 us
    sub x8, matrix products, block_probabilities(): exponentials = jnp.exp(scores - row_peak)  53.7 us
    unnamed x33, waiting for transfers between devices  44.9 us
  transfers between devices with their start and end apart: 36, of which 7 were waited for; matrix products, arithmetic and copies ran while one was open for 9% of the time, Pallas kernels for 0%

commit v1 on v0

--- a/solution.py
+++ b/solution.py
@@ -105,7 +105,8 @@
     standard = centered * inv_std
     normed = standard.astype(jnp.bfloat16)
     valid = jnp.arange(total_rows, dtype=jnp.int32) < length
-    weight_full = lax.all_gather(projection, "fsdp", axis=0, tiled=True)
+    repeated = jnp.stack([projection] * lax.axis_size("fsdp"))
+    weight_full = jnp.concatenate(lax.all_to_all(repeated, "fsdp", 0, 0), axis=0)
     packed = jnp.dot(normed, weight_full, preferred_element_type=jnp.float32).astype(jnp.bfloat16)
     packed = packed.reshape(local_rows, 3, seq_count, group_width)
     upstream_four = upstream.reshape(local_rows, 1, seq_count, group_width)

time: 1040 us -> 1080 us (1.038)
  waiting for transfers between devices: 127 us -> 170 us
  between operations: 15.5 us -> 2.07 us
    all_to_all x0 -> x1, waiting for transfers between devices: none -> 104 us  [body(): lax.all_to_all(repeated, 'fsdp', 0, 0)]
    all_gather x1 -> x0, waiting for transfers between devices: 61.9 us -> none  [body(): weight_full = lax.all_gather(projection, 'fsdp', axis=0, tiled=True)]
    unnamed x33 -> x37, local copies, waits for them, and re-layouts: 94 us -> 92.8 us
    unnamed x33 -> x32, waiting for transfers between devices: 44.9 us -> 44.1 us
  transfers between devices with their start and end apart: 36 -> 36, of which waited for: 7 -> 8; matrix products, arithmetic and copies ran while one was open for 9% -> 9% of each run, Pallas kernels for 0% -> 0%
where the time goes in v1:
time: 1080 us
  blocking collectives  355 us (33%)
  matrix products  254 us (24%)
  waiting for transfers between devices  170 us (16%)
  starting transfers between devices  139 us (13%)
  local copies, waits for them, and re-layouts  131 us (12%)
  other arithmetic  18.6 us (2%)
    unnamed x1, blocking collectives  326 us
    unnamed x32, starting transfers between devices  120 us
    all_to_all x1, waiting for transfers between devices, body(): lax.all_to_all(repeated, 'fsdp', 0, 0)  104 us
    unnamed x37, local copies, waits for them, and re-layouts  92.8 us
    dot_general x4, matrix products, backward_one_block(): jnp.einsum('hqk,qhd->khd', score_gradient, query_block, preferred_element...  62.9 us
    dot_general x4, matrix products, backward_one_block(): jnp.einsum('hqk,khd->qhd', score_gradient, key_rows, preferred_element_ty...  57.4 us
    sub x8, matrix products, block_probabilities(): exponentials = jnp.exp(scores - row_peak)  53.7 us
    unnamed x32, waiting for transfers between devices  44.1 us
  transfers between devices with their start and end apart: 36, of which 8 were waited for; matrix products, arithmetic and copies ran while one was open for 9% of the time, Pallas kernels for 0%

profile of v1, /device:TPU:2, one launch (start us, length us, event | category | flops | bytes accessed | tf_op | source)
XLA Modules:
  0.0 1075.5 jit_solution(946491165467172992)
XLA Ops:
  0.6 6.5 stack.18
  7.2 5.9 all-to-all-start
  14.7 104.3 %all-to-all-done = bf16[4,384,3072]{2,1,0:T(8,128)(2,1)} async-done(((bf16[4,384,3072]{2,1,0:T(8,128)(2,1)}), bf16[4,384,3072]{2,1,0:T(8,128)(2,1)}, u32[]{:S(2)}, u32[]{:S(2)}) %all-to-all-start) | async-done | bytes 9437216 | tf_op jit(solution)/shard_map/all_to_all | solution.py:109
  119.0 5.8 all-to-all-start.3
  124.8 6.4 fusion.104
  134.7 4.1 all-to-all-start.1
  140.0 19.6 %all-to-all-done.1 = bf16[256,3,8,128]{3,0,1,2:T(8,128)(2,1)S(1)} async-done(((bf16[256,3,8,128]{3,0,1,2:T(8,128)(2,1)}), bf16[256,3,8,128]{3,0,1,2:T(8,128)(2,1)S(1)}, u32[]{:S(2)}, u32[]{:S(2)}) %all-to-all-start.1) | async-done | bytes 1572896 | tf_op jit(solution)/shard_map/all_to_all | solution.py:114
  165.0 196.6 %while.26 = (s32[]{:T(128)}, f32[2048,2,64]{0,2,1:T(8,128)}, f32[2048,2,64]{0,2,1:T(8,128)}, bf16[4,512,2,64]{1,3,2,0:T(8,128)(2,1)S(1)}, s32[4]{0:T(128)S(1)}, ...) while((s32[]{:T(128)}, f32[2048,2,64]{0,2,1:T(8,128)}, ...), condition=%wide.region_10.11_spmd.clone, body=%wide.region_6.10_spmd.clone.sunk | while | flops 1385373696 | bytes 107115288 | solution.py:80
  166.4 4.6 fusion.162
  170.9 6.6 fusion.163
  177.5 14.4 %fusion.166 = bf16[4,512,2,64]{1,3,2,0:T(8,128)(2,1)S(1)} fusion(bf16[4,512,2,64]{1,3,2,0:T(8,128)(2,1)S(1)} %get-tuple-element.351, s32[]{:T(128)} %get-tuple-element.348, bf16[2048,2,64]{0,2,1:T(8,128)(2,1)S(1)} %get-tuple-element.369, f32[2,512,2048]{2,1,0:T(8,128)} %fusion.162, f32[2,512,2048]{2,1,0:T(8,128)} %get-tuple-element.299, ...), kind=kOutput, calls=%fused_computation.43.clone.1 | convolution fusion | flops 283184128 | bytes 34218496 | tf_op jit(solution)/shard_map/while/body/eval_jaxpr/hqk,khd->qhd/dot_general | solution.py:71
  191.9 5.4 fusion.165
  197.3 15.7 %fusion.164 = f32[2048,2,64]{0,2,1:T(8,128)S(1)} fusion(f32[2,512,2048]{2,1,0:T(8,128)} %fusion.162, f32[2048,2,64]{0,2,1:T(8,128)S(1)} %copy-done.2, pred[]{:T(512)S(6)} %compare.3, bf16[2048,2,64]{0,2,1:T(8,128)(2,1)} %get-tuple-element.367, s32[]{:T(128)S(6)} %select_n.71, f32[2,512,2048]{2,1,0:T(8,128)} %get-tuple-element.299, ...), kind=kOutput, calls=%fused_computation.40.clone.1 | convolution fusion | flops 283642880 | bytes 35790852 | tf_op jit(solution)/shard_map/while/body/eval_jaxpr/hqk,qhd->khd/dot_general | solution.py:74
  215.3 4.6 fusion.162
  219.9 6.6 fusion.163
  226.5 14.3 %fusion.166 = bf16[4,512,2,64]{1,3,2,0:T(8,128)(2,1)S(1)} fusion(bf16[4,512,2,64]{1,3,2,0:T(8,128)(2,1)S(1)} %get-tuple-element.351, s32[]{:T(128)} %get-tuple-element.348, bf16[2048,2,64]{0,2,1:T(8,128)(2,1)S(1)} %get-tuple-element.369, f32[2,512,2048]{2,1,0:T(8,128)} %fusion.162, f32[2,512,2048]{2,1,0:T(8,128)} %get-tuple-element.299, ...), kind=kOutput, calls=%fused_computation.43.clone.1 | convolution fusion | flops 283184128 | bytes 34218496 | tf_op jit(solution)/shard_map/while/body/eval_jaxpr/hqk,khd->qhd/dot_general | solution.py:71
  240.8 5.6 fusion.165
  246.5 15.7 %fusion.164 = f32[2048,2,64]{0,2,1:T(8,128)S(1)} fusion(f32[2,512,2048]{2,1,0:T(8,128)} %fusion.162, f32[2048,2,64]{0,2,1:T(8,128)S(1)} %copy-done.2, pred[]{:T(512)S(6)} %compare.3, bf16[2048,2,64]{0,2,1:T(8,128)(2,1)} %get-tuple-element.367, s32[]{:T(128)S(6)} %select_n.71, f32[2,512,2048]{2,1,0:T(8,128)} %get-tuple-element.299, ...), kind=kOutput, calls=%fused_computation.40.clone.1 | convolution fusion | flops 283642880 | bytes 35790852 | tf_op jit(solution)/shard_map/while/body/eval_jaxpr/hqk,qhd->khd/dot_general | solution.py:74
  264.5 4.6 fusion.162
  269.1 6.6 fusion.163
  275.7 14.4 %fusion.166 = bf16[4,512,2,64]{1,3,2,0:T(8,128)(2,1)S(1)} fusion(bf16[4,512,2,64]{1,3,2,0:T(8,128)(2,1)S(1)} %get-tuple-element.351, s32[]{:T(128)} %get-tuple-element.348, bf16[2048,2,64]{0,2,1:T(8,128)(2,1)S(1)} %get-tuple-element.369, f32[2,512,2048]{2,1,0:T(8,128)} %fusion.162, f32[2,512,2048]{2,1,0:T(8,128)} %get-tuple-element.299, ...), kind=kOutput, calls=%fused_computation.43.clone.1 | convolution fusion | flops 283184128 | bytes 34218496 | tf_op jit(solution)/shard_map/while/body/eval_jaxpr/hqk,khd->qhd/dot_general | solution.py:71
  290.1 5.6 fusion.165
  295.7 15.7 %fusion.164 = f32[2048,2,64]{0,2,1:T(8,128)S(1)} fusion(f32[2,512,2048]{2,1,0:T(8,128)} %fusion.162, f32[2048,2,64]{0,2,1:T(8,128)S(1)} %copy-done.2, pred[]{:T(512)S(6)} %compare.3, bf16[2048,2,64]{0,2,1:T(8,128)(2,1)} %get-tuple-element.367, s32[]{:T(128)S(6)} %select_n.71, f32[2,512,2048]{2,1,0:T(8,128)} %get-tuple-element.299, ...), kind=kOutput, calls=%fused_computation.40.clone.1 | convolution fusion | flops 283642880 | bytes 35790852 | tf_op jit(solution)/shard_map/while/body/eval_jaxpr/hqk,qhd->khd/dot_general | solution.py:74
  313.8 4.6 fusion.162
  318.3 6.6 fusion.163
  324.9 14.4 %fusion.166 = bf16[4,512,2,64]{1,3,2,0:T(8,128)(2,1)S(1)} fusion(bf16[4,512,2,64]{1,3,2,0:T(8,128)(2,1)S(1)} %get-tuple-element.351, s32[]{:T(128)} %get-tuple-element.348, bf16[2048,2,64]{0,2,1:T(8,128)(2,1)S(1)} %get-tuple-element.369, f32[2,512,2048]{2,1,0:T(8,128)} %fusion.162, f32[2,512,2048]{2,1,0:T(8,128)} %get-tuple-element.299, ...), kind=kOutput, calls=%fused_computation.43.clone.1 | convolution fusion | flops 283184128 | bytes 34218496 | tf_op jit(solution)/shard_map/while/body/eval_jaxpr/hqk,khd->qhd/dot_general | solution.py:71
  339.3 5.6 fusion.165
  344.9 15.7 %fusion.164 = f32[2048,2,64]{0,2,1:T(8,128)S(1)} fusion(f32[2,512,2048]{2,1,0:T(8,128)} %fusion.162, f32[2048,2,64]{0,2,1:T(8,128)S(1)} %copy-done.2, pred[]{:T(512)S(6)} %compare.3, bf16[2048,2,64]{0,2,1:T(8,128)(2,1)} %get-tuple-element.367, s32[]{:T(128)S(6)} %select_n.71, f32[2,512,2048]{2,1,0:T(8,128)} %get-tuple-element.299, ...), kind=kOutput, calls=%fused_computation.40.clone.1 | convolution fusion | flops 283642880 | bytes 35790852 | tf_op jit(solution)/shard_map/while/body/eval_jaxpr/hqk,qhd->khd/dot_general | solution.py:74
  366.4 3.0 copy.54
  369.4 29.5 %all_to_all.65 = bf16[2048,3,1,128]{3,1,2,0:T(4,128)(2,1)S(1)} all-to-all(bf16[2048,3,1,128]{3,1,2,0:T(4,128)(2,1)S(1)} %copy.54), channel_id=1, replica_groups=mesh['dp'=4,'fsdp'=4,'seq'=8] {'seq'}, dimensions={0} | all-to-all | bytes 3145728 | tf_op jit(solution)/shard_map/all_to_all | solution.py:133
  402.0 8.0 fusion.106
  410.1 325.8 %fusion = f32[16,3072]{1,0:T(8,128)} fusion(f32[1536,3072]{1,0:T(8,128)} %fusion.106), kind=kCustom, calls=%all-reduce-scatter | all-reduce-scatter fusion | flops 6291457 | bytes 19070976
  735.9 3.2 collective-permute-start
  740.0 3.6 collective-permute-start.31
  743.6 3.1 collective-permute-start.1
  748.6 7.0 collective-permute-start.11
  755.7 33.1 %collective-permute-done.31 = f32[12,3072]{1,0:T(8,128)S(1)} collective-permute-done((f32[12,3072]{1,0:T(8,128)S(1)}, f32[12,3072]{1,0:T(8,128)S(1)}, u32[]{:S(2)}, u32[]{:S(2)}) %collective-permute-start.31) | collective-permute-done | bytes 147488
  792.9 52.5 %while.25 = (s32[]{:T(128)}, bf16[4,512,2,64]{1,3,2,0:T(8,128)(2,1)S(1)}, s32[4]{0:T(128)S(1)}, pred[2048]{0:T(1024)(128)(4,1)S(1)}, bf16[2048,2,64]{0,2,1:T(8,1...) while((s32[]{:T(128)}, ...), condition=%wide.region_5.6_spmd, body=%wide.region_2.5_spmd.sunk | while | flops 549586944 | bytes 18099892 | solution.py:42
  794.3 6.8 fusion.152
  801.2 4.8 fusion.153
  807.4 6.8 fusion.152
  814.3 4.8 fusion.153
  820.5 6.8 fusion.152
  827.4 4.8 fusion.153
  833.6 6.8 fusion.152
  840.5 4.8 fusion.153
  847.4 5.0 reshape.103
  852.9 12.6 %reduce.1 = bf16[2048,128]{1,0:T(8,128)(2,1)S(1)} reduce(bf16[2048,1,128]{2,1,0:T(2,128)(2,1)} %reshape.103, bf16[]{:T(256)} %broadcast.131), dimensions={1}, to_apply=%reshape.103.reduce_sub_computation | reduce | bytes 1048578 | tf_op jit(solution)/shard_map/reshape;reshape | solution.py:124
  866.4 3.5 all-to-all-start.2
  869.9 12.5 %collective-permute-start.14 = (f32[16,3072]{1,0:T(8,128)}, f32[16,3072]{1,0:T(8,128)}, u32[]{:S(2)}, u32[]{:S(2)}) collective-permute-start(f32[16,3072]{1,0:T(8,128)} %fusion), channel_id=1, source_target_pairs={{0,15},{1,16},{2,17},{3,18},{4,19},{5,20},{6,21},{7,22},{8,23},{9,... | collective-permute-start | bytes 589832
  884.3 3.9 collective-permute-start.16
  888.3 4.9 collective-permute-start.17
  897.3 10.0 collective-permute-start.2
  907.3 5.8 collective-permute-start.20
  913.1 5.6 collective-permute-start.21
  929.0 5.5 collective-permute-start.25
  938.7 5.5 fusion.109
  948.1 2.8 collective-permute-start.3
  957.6 6.1 collective-permute-start.5
  963.7 4.9 collective-permute-start.6
  968.6 3.9 collective-permute-start.7
  974.5 5.6 collective-permute-start.9
  981.7 6.3 collective-permute-done.8
  990.0 83.8 %concatenate.1 = f32[524,3072]{1,0:T(8,128)} concatenate(f32[12,3072]{1,0:T(8,128)S(1)} %copy-done.9, f32[16,3072]{1,0:T(8,128)S(1)} %collective-permute-done.30, f32[16,3072]{1,0:T(8,128)S(1)} %collective-permute-done.29, f32[16,3072]{1,0:T(8,128)S(1)} %collective-permute-done.28, f32[16,3072]{1,0:T(8,128)} %copy-done.11, f32[16,3072]{1,0:T(8,128)} %copy-done.10, ...), dimensions={0} | concatenate | bytes 12877824
  (145 shorter events, 76.8 us)
Async XLA Ops:
  7.2 5.9 copy-start.4
  7.2 6.9 copy-start
  7.2 111.9 %all-to-all-start = ((bf16[4,384,3072]{2,1,0:T(8,128)(2,1)}), bf16[4,384,3072]{2,1,0:T(8,128)(2,1)}, u32[]{:S(2)}, u32[]{:S(2)}) async-start(bf16[4,384,3072]{2,1,0:T(8,128)(2,1)} %stack.18), calls=%async_computation | async-start | bytes 18874368 | tf_op jit(solution)/shard_map/all_to_all | solution.py:109
  14.3 116.9 %copy-start.12 = (f32[256]{0:T(256)}, f32[256]{0:T(256)S(1)}, u32[]{:S(2)}) copy-start(f32[256]{0:T(256)S(1)} %broadcast_multiply_fusion.2) | copy-start | bytes 3076
  14.7 116.6 %copy-start.14 = (f32[256]{0:T(256)}, f32[256]{0:T(256)S(1)}, u32[]{:S(2)}) copy-start(f32[256]{0:T(256)S(1)} %add_rsqrt_fusion) | copy-start | bytes 3076
  119.0 15.7 %all-to-all-start.3 = ((bf16[256,1,8,128]{0,3,1,2:T(8,128)(2,1)}), bf16[256,1,8,128]{0,3,1,2:T(8,128)(2,1)S(1)}, u32[]{:S(2)}, u32[]{:S(2)}) async-start(bf16[256,1,8,128]{0,3,1,2:T(8,128)(2,1)} %bitcast.14), calls=%async_computation.3 | async-start | bytes 1048576 | tf_op jit(solution)/shard_map/all_to_all | solution.py:115
  134.7 24.9 %all-to-all-start.1 = ((bf16[256,3,8,128]{3,0,1,2:T(8,128)(2,1)}), bf16[256,3,8,128]{3,0,1,2:T(8,128)(2,1)S(1)}, u32[]{:S(2)}, u32[]{:S(2)}) async-start(bf16[256,3,8,128]{3,0,1,2:T(8,128)(2,1)} %copy.46), calls=%async_computation.1 | async-start | bytes 3145728 | tf_op jit(solution)/shard_map/all_to_all | solution.py:114
  191.9 5.4 copy-start.2
  213.0 1.0 copy-start.3
  240.8 5.6 copy-start.2
  262.2 1.0 copy-start.3
  290.1 5.6 copy-start.2
  311.4 1.0 copy-start.3
  339.3 5.6 copy-start.2
  360.7 1.0 copy-start.3
  361.7 3.4 copy-start.5
  365.1 36.9 %copy-start.1 = (bf16[1,256,1536]{2,1,0:T(8,128)(2,1)S(1)}, bf16[1,256,1536]{2,1,0:T(8,128)(2,1)}, u32[]{:S(2)}) copy-start(bf16[1,256,1536]{2,1,0:T(8,128)(2,1)} %param.8) | copy-start | bytes 2359300
  365.1 36.9 %copy-start.13 = (f32[256]{0:T(256)S(1)}, f32[256]{0:T(256)}, u32[]{:S(2)}) copy-start(f32[256]{0:T(256)} %copy-done.12) | copy-start | bytes 3076
  365.1 36.9 %copy-start.15 = (f32[256]{0:T(256)S(1)}, f32[256]{0:T(256)}, u32[]{:S(2)}) copy-start(f32[256]{0:T(256)} %copy-done.14) | copy-start | bytes 3076
  735.9 54.8 %collective-permute-start = (f32[16,3072]{1,0:T(8,128)}, f32[16,3072]{1,0:T(8,128)S(1)}, u32[]{:S(2)}, u32[]{:S(2)}) collective-permute-start(f32[16,3072]{1,0:T(8,128)} %fusion), channel_id=1, source_target_pairs={{0,1},{1,2},{2,3},{3,4},{4,5},{5,6},{6,7},{7,8},{8,9},{9,10},{10,1... | collective-permute-start | bytes 589832
  740.0 48.7 %collective-permute-start.31 = (f32[12,3072]{1,0:T(8,128)S(1)}, f32[12,3072]{1,0:T(8,128)S(1)}, u32[]{:S(2)}, u32[]{:S(2)}) collective-permute-start(f32[12,3072]{1,0:T(8,128)S(1)} %slice.15), channel_id=1, source_target_pairs={{0,32},{1,33},{2,34},{3,35},{4,36},{5,37},{6,38},{7,39},{8,40},{9,... | collective-permute-start | bytes 442376
  743.6 126.3 %collective-permute-start.1 = (f32[16,3072]{1,0:T(8,128)}, f32[16,3072]{1,0:T(8,128)}, u32[]{:S(2)}, u32[]{:S(2)}) collective-permute-start(f32[16,3072]{1,0:T(8,128)} %fusion), channel_id=1, source_target_pairs={{0,2},{1,3},{2,4},{3,5},{4,6},{5,7},{6,8},{7,9},{8,10},{9,11},{10,... | collective-permute-start | bytes 589832
  746.7 135.7 %collective-permute-start.10 = (f32[16,3072]{1,0:T(8,128)}, f32[16,3072]{1,0:T(8,128)}, u32[]{:S(2)}, u32[]{:S(2)}) collective-permute-start(f32[16,3072]{1,0:T(8,128)} %fusion), channel_id=1, source_target_pairs={{0,11},{1,12},{2,13},{3,14},{4,15},{5,16},{6,17},{7,18},{8,19},{9,... | collective-permute-start | bytes 589832
  748.6 135.7 %collective-permute-start.11 = (f32[16,3072]{1,0:T(8,128)}, f32[16,3072]{1,0:T(8,128)}, u32[]{:S(2)}, u32[]{:S(2)}) collective-permute-start(f32[16,3072]{1,0:T(8,128)} %fusion), channel_id=1, source_target_pairs={{0,12},{1,13},{2,14},{3,15},{4,16},{5,17},{6,18},{7,19},{8,20},{9,... | collective-permute-start | bytes 589832
  788.7 4.1 copy-start.8
  788.7 99.5 %collective-permute-start.12 = (f32[16,3072]{1,0:T(8,128)}, f32[16,3072]{1,0:T(8,128)}, u32[]{:S(2)}, u32[]{:S(2)}) collective-permute-start(f32[16,3072]{1,0:T(8,128)} %fusion), channel_id=1, source_target_pairs={{0,13},{1,14},{2,15},{3,16},{4,17},{5,18},{6,19},{7,20},{8,21},{9,... | collective-permute-start | bytes 589832
  790.7 2.2 copy-start.6
  790.7 102.5 %collective-permute-start.13 = (f32[16,3072]{1,0:T(8,128)}, f32[16,3072]{1,0:T(8,128)}, u32[]{:S(2)}, u32[]{:S(2)}) collective-permute-start(f32[16,3072]{1,0:T(8,128)} %fusion), channel_id=1, source_target_pairs={{0,14},{1,15},{2,16},{3,17},{4,18},{5,19},{6,20},{7,21},{8,22},{9,... | collective-permute-start | bytes 589832
  866.4 54.3 %all-to-all-start.2 = ((bf16[8,2,16384]{2,1,0:T(2,128)(2,1)}), bf16[8,2,16384]{2,1,0:T(2,128)(2,1)S(1)}, u32[]{:S(2)}, u32[]{:S(2)}) async-start(bf16[8,2,16384]{2,1,0:T(2,128)(2,1)} %reshape.104), calls=%async_computation.2 | async-start | bytes 1048576 | tf_op jit(solution)/shard_map/all_to_all | solution.py:123
  869.9 25.5 %collective-permute-start.14 = (f32[16,3072]{1,0:T(8,128)}, f32[16,3072]{1,0:T(8,128)}, u32[]{:S(2)}, u32[]{:S(2)}) collective-permute-start(f32[16,3072]{1,0:T(8,128)} %fusion), channel_id=1, source_target_pairs={{0,15},{1,16},{2,17},{3,18},{4,19},{5,20},{6,21},{7,22},{8,23},{9,... | collective-permute-start | bytes 589832
  882.4 15.0 %collective-permute-start.15 = (f32[16,3072]{1,0:T(8,128)}, f32[16,3072]{1,0:T(8,128)}, u32[]{:S(2)}, u32[]{:S(2)}) collective-permute-start(f32[16,3072]{1,0:T(8,128)} %fusion), channel_id=1, source_target_pairs={{0,16},{1,17},{2,18},{3,19},{4,20},{5,21},{6,22},{7,23},{8,24},{9,... | collective-permute-start | bytes 589832
  884.3 23.0 %collective-permute-start.16 = (f32[16,3072]{1,0:T(8,128)}, f32[16,3072]{1,0:T(8,128)}, u32[]{:S(2)}, u32[]{:S(2)}) collective-permute-start(f32[16,3072]{1,0:T(8,128)} %fusion), channel_id=1, source_target_pairs={{0,17},{1,18},{2,19},{3,20},{4,21},{5,22},{6,23},{7,24},{8,25},{9,... | collective-permute-start | bytes 589832
  888.3 24.9 %collective-permute-start.17 = (f32[16,3072]{1,0:T(8,128)}, f32[16,3072]{1,0:T(8,128)}, u32[]{:S(2)}, u32[]{:S(2)}) collective-permute-start(f32[16,3072]{1,0:T(8,128)} %fusion), channel_id=1, source_target_pairs={{0,18},{1,19},{2,20},{3,21},{4,22},{5,23},{6,24},{7,25},{8,26},{9,... | collective-permute-start | bytes 589832
  893.1 25.6 %collective-permute-start.18 = (f32[16,3072]{1,0:T(8,128)}, f32[16,3072]{1,0:T(8,128)}, u32[]{:S(2)}, u32[]{:S(2)}) collective-permute-start(f32[16,3072]{1,0:T(8,128)} %fusion), channel_id=1, source_target_pairs={{0,19},{1,20},{2,21},{3,22},{4,23},{5,24},{6,25},{7,26},{8,27},{9,... | collective-permute-start | bytes 589832
  895.4 29.6 %collective-permute-start.19 = (f32[16,3072]{1,0:T(8,128)}, f32[16,3072]{1,0:T(8,128)}, u32[]{:S(2)}, u32[]{:S(2)}) collective-permute-start(f32[16,3072]{1,0:T(8,128)} %fusion), channel_id=1, source_target_pairs={{0,20},{1,21},{2,22},{3,23},{4,24},{5,25},{6,26},{7,27},{8,28},{9,... | collective-permute-start | bytes 589832
  897.3 29.7 %collective-permute-start.2 = (f32[16,3072]{1,0:T(8,128)}, f32[16,3072]{1,0:T(8,128)}, u32[]{:S(2)}, u32[]{:S(2)}) collective-permute-start(f32[16,3072]{1,0:T(8,128)} %fusion), channel_id=1, source_target_pairs={{0,3},{1,4},{2,5},{3,6},{4,7},{5,8},{6,9},{7,10},{8,11},{9,12},{10... | collective-permute-start | bytes 589832
  907.3 21.7 %collective-permute-start.20 = (f32[16,3072]{1,0:T(8,128)}, f32[16,3072]{1,0:T(8,128)}, u32[]{:S(2)}, u32[]{:S(2)}) collective-permute-start(f32[16,3072]{1,0:T(8,128)} %fusion), channel_id=1, source_target_pairs={{0,21},{1,22},{2,23},{3,24},{4,25},{5,26},{6,27},{7,28},{8,29},{9,... | collective-permute-start | bytes 589832
  913.1 21.4 %collective-permute-start.21 = (f32[16,3072]{1,0:T(8,128)}, f32[16,3072]{1,0:T(8,128)}, u32[]{:S(2)}, u32[]{:S(2)}) collective-permute-start(f32[16,3072]{1,0:T(8,128)} %fusion), channel_id=1, source_target_pairs={{0,22},{1,23},{2,24},{3,25},{4,26},{5,27},{6,28},{7,29},{8,30},{9,... | collective-permute-start | bytes 589832
  918.7 17.7 %collective-permute-start.22 = (f32[16,3072]{1,0:T(8,128)}, f32[16,3072]{1,0:T(8,128)}, u32[]{:S(2)}, u32[]{:S(2)}) collective-permute-start(f32[16,3072]{1,0:T(8,128)} %fusion), channel_id=1, source_target_pairs={{0,23},{1,24},{2,25},{3,26},{4,27},{5,28},{6,29},{7,30},{8,31},{9,... | collective-permute-start | bytes 589832
  925.0 65.0 %copy-start.7 = (f32[16,3072]{1,0:T(8,128)S(1)}, f32[16,3072]{1,0:T(8,128)}, u32[]{:S(2)}) copy-start(f32[16,3072]{1,0:T(8,128)} %copy-done.6) | copy-start | bytes 589828
  925.0 65.0 %copy-start.9 = (f32[12,3072]{1,0:T(8,128)S(1)}, f32[12,3072]{1,0:T(8,128)}, u32[]{:S(2)}) copy-start(f32[12,3072]{1,0:T(8,128)} %copy-done.8) | copy-start | bytes 442372
  925.0 19.2 %collective-permute-start.23 = (f32[16,3072]{1,0:T(8,128)}, f32[16,3072]{1,0:T(8,128)S(1)}, u32[]{:S(2)}, u32[]{:S(2)}) collective-permute-start(f32[16,3072]{1,0:T(8,128)} %fusion), channel_id=1, source_target_pairs={{0,24},{1,25},{2,26},{3,27},{4,28},{5,29},{6,30},{7,31},{8,32},{9,... | collective-permute-start | bytes 589832
  927.1 19.0 %collective-permute-start.24 = (f32[16,3072]{1,0:T(8,128)}, f32[16,3072]{1,0:T(8,128)S(1)}, u32[]{:S(2)}, u32[]{:S(2)}) collective-permute-start(f32[16,3072]{1,0:T(8,128)} %fusion), channel_id=1, source_target_pairs={{0,25},{1,26},{2,27},{3,28},{4,29},{5,30},{6,31},{7,32},{8,33},{9,... | collective-permute-start | bytes 589832
  929.0 19.0 %collective-permute-start.25 = (f32[16,3072]{1,0:T(8,128)}, f32[16,3072]{1,0:T(8,128)S(1)}, u32[]{:S(2)}, u32[]{:S(2)}) collective-permute-start(f32[16,3072]{1,0:T(8,128)} %fusion), channel_id=1, source_target_pairs={{0,26},{1,27},{2,28},{3,29},{4,30},{5,31},{6,32},{7,33},{8,34},{9,... | collective-permute-start | bytes 589832
  934.5 16.6 %collective-permute-start.26 = (f32[16,3072]{1,0:T(8,128)}, f32[16,3072]{1,0:T(8,128)S(1)}, u32[]{:S(2)}, u32[]{:S(2)}) collective-permute-start(f32[16,3072]{1,0:T(8,128)} %fusion), channel_id=1, source_target_pairs={{0,27},{1,28},{2,29},{3,30},{4,31},{5,32},{6,33},{7,34},{8,35},{9,... | collective-permute-start | bytes 589832
  936.5 16.6 %collective-permute-start.27 = (f32[16,3072]{1,0:T(8,128)}, f32[16,3072]{1,0:T(8,128)S(1)}, u32[]{:S(2)}, u32[]{:S(2)}) collective-permute-start(f32[16,3072]{1,0:T(8,128)} %fusion), channel_id=1, source_target_pairs={{0,28},{1,29},{2,30},{3,31},{4,32},{5,33},{6,34},{7,35},{8,36},{9,... | collective-permute-start | bytes 589832
  944.2 13.4 %collective-permute-start.28 = (f32[16,3072]{1,0:T(8,128)}, f32[16,3072]{1,0:T(8,128)S(1)}, u32[]{:S(2)}, u32[]{:S(2)}) collective-permute-start(f32[16,3072]{1,0:T(8,128)} %fusion), channel_id=1, source_target_pairs={{0,29},{1,30},{2,31},{3,32},{4,33},{5,34},{6,35},{7,36},{8,37},{9,... | collective-permute-start | bytes 589832
  946.1 17.6 %collective-permute-start.29 = (f32[16,3072]{1,0:T(8,128)}, f32[16,3072]{1,0:T(8,128)S(1)}, u32[]{:S(2)}, u32[]{:S(2)}) collective-permute-start(f32[16,3072]{1,0:T(8,128)} %fusion), channel_id=1, source_target_pairs={{0,30},{1,31},{2,32},{3,33},{4,34},{5,35},{6,36},{7,37},{8,38},{9,... | collective-permute-start | bytes 589832
  948.1 20.6 %collective-permute-start.3 = (f32[16,3072]{1,0:T(8,128)}, f32[16,3072]{1,0:T(8,128)S(1)}, u32[]{:S(2)}, u32[]{:S(2)}) collective-permute-start(f32[16,3072]{1,0:T(8,128)} %fusion), channel_id=1, source_target_pairs={{0,4},{1,5},{2,6},{3,7},{4,8},{5,9},{6,10},{7,11},{8,12},{9,13},{1... | collective-permute-start | bytes 589832
  951.2 30.5 %copy-start.10 = (f32[16,3072]{1,0:T(8,128)}, f32[16,3072]{1,0:T(8,128)S(1)}, u32[]{:S(2)}) copy-start(f32[16,3072]{1,0:T(8,128)S(1)} %collective-permute-done.26) | copy-start | bytes 589828
  951.2 21.4 %collective-permute-start.30 = (f32[16,3072]{1,0:T(8,128)}, f32[16,3072]{1,0:T(8,128)S(1)}, u32[]{:S(2)}, u32[]{:S(2)}) collective-permute-start(f32[16,3072]{1,0:T(8,128)} %fusion), channel_id=1, source_target_pairs={{0,31},{1,32},{2,33},{3,34},{4,35},{5,36},{6,37},{7,38},{8,39},{9,... | collective-permute-start | bytes 589832
  953.1 28.6 %copy-start.11 = (f32[16,3072]{1,0:T(8,128)}, f32[16,3072]{1,0:T(8,128)S(1)}, u32[]{:S(2)}) copy-start(f32[16,3072]{1,0:T(8,128)S(1)} %collective-permute-done.27) | copy-start | bytes 589828
  953.1 21.4 %collective-permute-start.4 = (f32[16,3072]{1,0:T(8,128)}, f32[16,3072]{1,0:T(8,128)S(1)}, u32[]{:S(2)}, u32[]{:S(2)}) collective-permute-start(f32[16,3072]{1,0:T(8,128)} %fusion), channel_id=1, source_target_pairs={{0,5},{1,6},{2,7},{3,8},{4,9},{5,10},{6,11},{7,12},{8,13},{9,14},{... | collective-permute-start | bytes 589832
  957.6 24.1 %collective-permute-start.5 = (f32[16,3072]{1,0:T(8,128)}, f32[16,3072]{1,0:T(8,128)S(1)}, u32[]{:S(2)}, u32[]{:S(2)}) collective-permute-start(f32[16,3072]{1,0:T(8,128)} %fusion), channel_id=1, source_target_pairs={{0,6},{1,7},{2,8},{3,9},{4,10},{5,11},{6,12},{7,13},{8,14},{9,15},... | collective-permute-start | bytes 589832
  963.7 18.0 %collective-permute-start.6 = (f32[16,3072]{1,0:T(8,128)}, f32[16,3072]{1,0:T(8,128)S(1)}, u32[]{:S(2)}, u32[]{:S(2)}) collective-permute-start(f32[16,3072]{1,0:T(8,128)} %fusion), channel_id=1, source_target_pairs={{0,7},{1,8},{2,9},{3,10},{4,11},{5,12},{6,13},{7,14},{8,15},{9,16}... | collective-permute-start | bytes 589832
  968.6 13.1 %collective-permute-start.7 = (f32[16,3072]{1,0:T(8,128)}, f32[16,3072]{1,0:T(8,128)S(1)}, u32[]{:S(2)}, u32[]{:S(2)}) collective-permute-start(f32[16,3072]{1,0:T(8,128)} %fusion), channel_id=1, source_target_pairs={{0,8},{1,9},{2,10},{3,11},{4,12},{5,13},{6,14},{7,15},{8,16},{9,17... | collective-permute-start | bytes 589832
  972.6 15.5 %collective-permute-start.8 = (f32[16,3072]{1,0:T(8,128)}, f32[16,3072]{1,0:T(8,128)}, u32[]{:S(2)}, u32[]{:S(2)}) collective-permute-start(f32[16,3072]{1,0:T(8,128)} %fusion), channel_id=1, source_target_pairs={{0,9},{1,10},{2,11},{3,12},{4,13},{5,14},{6,15},{7,16},{8,17},{9,1... | collective-permute-start | bytes 589832
  974.5 15.5 %collective-permute-start.9 = (f32[16,3072]{1,0:T(8,128)}, f32[16,3072]{1,0:T(8,128)}, u32[]{:S(2)}, u32[]{:S(2)}) collective-permute-start(f32[16,3072]{1,0:T(8,128)} %fusion), channel_id=1, source_target_pairs={{0,10},{1,11},{2,12},{3,13},{4,14},{5,15},{6,16},{7,17},{8,18},{9,... | collective-permute-start | bytes 589832
